TPU v7x, 512 devices: a whole 4x8x8 slice. The times are simulated.
512 devices in a mesh: grp: 8 (over y_hi, core), fsdp: 64 (over z, x, y_lo).
Axes of the slice: x: 4, y: 8 (y_hi: 4, y_lo: 2; y = y_hi * 2 + y_lo), z: 8, core: 2. Of those that a mesh axis runs over, the one named last changes fastest.
Arguments:
- hidden_in: bfloat16 [64, 8, 224, 2560], P('fsdp', 'grp'), may hold values from -16 to 16
- queries: bfloat16 [64, 8, 224, 2560], P('fsdp', 'grp'), may hold values from -5 to 5
- keys: bfloat16 [64, 8, 224, 512], P('fsdp', 'grp'), may hold values from -5 to 5
- logp_grad: bfloat16 [64, 8, 224, 2560], P('fsdp', 'grp'), may hold values from -96 to 96
- lengths: int32 [64, 8], P('fsdp', 'grp'), may hold values from 28 to 224, as said below
- rewards: int32 [64, 8], P('fsdp', 'grp'), may hold values from 0 to 3
- w_value: bfloat16 [2560, 512], P('fsdp'), may hold values from -1 to 1
Outputs:
- grad_weight: float32 [2560, 512], P('fsdp', 'grp')
- grad_input: bfloat16 [64, 8, 224, 2560], P('fsdp', 'grp')
Inputs may be any that keep to these rules, and one draw needn't show every extreme that they name: `lengths`: every prompt has one response of exactly 224 tokens; the others have at least 28.
All inputs are finite; a program needn't handle non-finite values.
Results may differ from a plain program's by a relative error of at most 0.015.
Values may be sent and summed in bfloat16 or wider, within the bound.
A program may use at most 64 MiB of HBM per device.

v0:
```python
import jax
import jax.numpy as jnp
from jax import lax
from jax.sharding import PartitionSpec as P

KV_HEADS = 4
RATIO = 5
HEAD_WIDTH = 128


def value_cotangent(queries, keys, logp_grad, factor, length):
    seq_len = queries.shape[0]
    query_head_rows = queries.reshape(seq_len, KV_HEADS, RATIO, HEAD_WIDTH)
    key_head_rows = keys.reshape(seq_len, KV_HEADS, HEAD_WIDTH)
    attention_logits = jnp.einsum(
        "wzhl,kzl->zhwk", query_head_rows, key_head_rows, preferred_element_type=jnp.float32
    ) * HEAD_WIDTH ** (-0.5)
    positions = jnp.arange(seq_len)
    causal = positions[:, None] >= positions[None, :]
    attention_logits = jnp.where(causal, attention_logits, -1e30)
    shifted = jnp.exp(attention_logits - jnp.max(attention_logits, axis=-1, keepdims=True))
    attention_probability = (shifted / jnp.sum(shifted, axis=-1, keepdims=True)).astype(
        jnp.bfloat16
    )
    weights = jnp.where(positions < length, factor, 0.0)
    scaled_scores = (logp_grad.astype(jnp.float32) * weights[:, None]).astype(jnp.bfloat16)
    scaled_scores = scaled_scores.reshape(seq_len, KV_HEADS, RATIO, HEAD_WIDTH)
    value_vectors = jnp.einsum(
        "zibl,bziq->lzq", attention_probability, scaled_scores, preferred_element_type=jnp.float32
    )
    return value_vectors.astype(jnp.bfloat16).reshape(seq_len, KV_HEADS * HEAD_WIDTH)


def local(hidden_in, queries, keys, logp_grad, lengths, rewards, w_value):
    members = lax.axis_size("grp")
    length = lengths[0, 0]
    reward = rewards[0, 0].astype(jnp.float32)
    summed, squares = lax.psum((reward, reward * reward), "grp")
    average = summed / members
    second = squares / members
    spread = jnp.maximum(jnp.sqrt(second - average * average), 1.0)
    advantage = (reward - average) / spread
    factor = -advantage / (members * length.astype(jnp.float32))
    inputs = hidden_in[0, 0]
    value_grad = value_cotangent(queries[0, 0], keys[0, 0], logp_grad[0, 0], factor, length)
    seq_len = inputs.shape[0]
    partial_grad = lax.dot_general(
        inputs, value_grad, (((0,), (0,)), ((), ())), preferred_element_type=jnp.float32
    )
    group_part = lax.psum_scatter(
        partial_grad.astype(jnp.bfloat16), "grp", scatter_dimension=1, tiled=True
    ).astype(jnp.float32)
    gradient = lax.psum_scatter(group_part, "fsdp", scatter_dimension=0, tiled=True)
    input_grad = lax.dot_general(
        value_grad,
        lax.all_gather(w_value, "fsdp", axis=0, tiled=True),
        (((1,), (1,)), ((), ())),
        preferred_element_type=jnp.float32,
    )
    grad_input = input_grad.astype(jnp.bfloat16).reshape(1, 1, seq_len, input_grad.shape[1])
    return (gradient, grad_input)


def solution(mesh):
    placed = (
        P("fsdp", "grp", None, None),
        P("fsdp", "grp", None, None),
        P("fsdp", "grp", None, None),
        P("fsdp", "grp", None, None),
        P("fsdp", "grp"),
        P("fsdp", "grp"),
        P("fsdp", None),
    )
    return jax.shard_map(
        local,
        mesh=mesh,
        in_specs=placed,
        out_specs=(P("fsdp", "grp"), P("fsdp", "grp", None, None)),
        check_vma=False,
    )
```

profile of v0, /device:TPU:16, one launch (start us, length us, event | category | flops | bytes accessed | tf_op | source)
XLA Modules:
  0.0 656.5 jit_solution(10370849375801622465)
XLA Ops:
  8.0 0.0 copy-start
  8.0 0.0 copy-start.1
  8.0 0.0 all-gather.2.cloned.1.call-start
  8.1 0.7 all-gather.2.cloned.1.call-update
  8.8 0.0 reduce-scatter.3.cloned.1.call-start
  9.5 16.7 %all-reduce.1 = (f32[]{:T(128)}, f32[]{:T(128)}) all-reduce(f32[]{:T(128)} %bitcast.2, f32[]{:T(128)S(6)} %mul.29), channel_id=1, replica_groups=mesh['grp'=8,'fsdp'=64] {'grp'}, use_global_device_ids=true, to_apply=%region_0.0 | all-reduce | flops 2 | bytes 16 | tf_op jit(solution)/shard_map/psum | solution.py:38
  29.5 1.6 copy.21
  31.1 0.0 copy-done.1
  31.1 0.1 reshape_squeeze.6
  31.2 2.9 copy.20
  34.1 3.7 fusion.28
  37.8 3.9 fusion.11
  41.7 0.0 copy-done
  41.7 2.4 fusion.1
  44.1 0.0 reduce-scatter.3.cloned.1.call-update
  44.1 1.3 dynamic-slice
  46.1 281.7 %all-gather.2.cloned.1.call-done = bf16[2560,512]{1,0:T(8,128)(2,1)} async-done(((bf16[40,512]{1,0:T(8,128)(2,1)}), bf16[2560,512]{1,0:T(8,128)(2,1)}) %all-gather.2.cloned.1.call-update) | async-done | bytes 2621456 | tf_op jit(solution)/shard_map/all_gather | solution.py:56
  327.8 3.7 fusion.2
  331.5 0.0 reduce-scatter.3.cloned.1.call-done
  331.5 316.7 %all-reduce.3 = f32[2560,64]{0,1:T(8,128)S(1)} all-reduce(bf16[2560,64]{0,1:T(8,128)(2,1)} %reduce-scatter.3.cloned.1.call-done), channel_id=3, replica_groups=mesh['grp'=8,'fsdp'=64] {'fsdp'}, use_global_device_ids=true, to_apply=%region_5.6.clone | all-reduce | flops 163840 | bytes 983040
  648.2 0.1 constant_dynamic-slice_fusion
  648.3 0.7 copy.26
  (2 shorter events, 0.0 us)
Async XLA Ops:
  8.0 33.7 %copy-start = (bf16[1,1,224,2560]{3,2,1,0:T(8,128)(2,1)S(1)}, bf16[1,1,224,2560]{3,2,1,0:T(8,128)(2,1)}, u32[]{:S(2)}) copy-start(bf16[1,1,224,2560]{3,2,1,0:T(8,128)(2,1)} %param.7) | copy-start | bytes 3440644
  8.0 23.1 %copy-start.1 = (bf16[1,1,224,512]{3,2,1,0:T(8,128)(2,1)S(1)}, bf16[1,1,224,512]{3,2,1,0:T(8,128)(2,1)}, u32[]{:S(2)}) copy-start(bf16[1,1,224,512]{3,2,1,0:T(8,128)(2,1)} %param.9) | copy-start | bytes 688132
  8.0 319.8 %all-gather.2.cloned.1.call-start = ((), (), s32[]{:S(2)}) async-start(), calls=%async_computation.2 | async-start | bytes 2662400 | tf_op jit(solution)/shard_map/all_gather | solution.py:56
  8.8 322.7 %reduce-scatter.3.cloned.1.call-start = ((), (), s32[]{:S(2)}) async-start(), calls=%async_computation.1 | async-start | bytes 2949120 | tf_op jit(solution)/shard_map/reduce_scatter | solution.py:50
Sparse Core Ops, SparseCore 0:
  10.9 316.8 all-gather.1
Sparse Core Ops, SparseCore 1:
  44.2 51.1 reduce-scatter.2
where the time goes:
time: 657 us; the launch traced here: 656 us
  blocking collectives  333 us (51%)
  waiting for transfers between devices  282 us (43%)
  between operations  20.3 us (3%)
  matrix products  13.6 us (2%)
    unnamed x1, blocking collectives  317 us
    all_gather x1, waiting for transfers between devices, local(): lax.all_gather(w_value, 'fsdp', axis=0, tiled=True)  282 us
    psum x1, blocking collectives, local(): summed, squares = lax.psum((reward, reward * reward), 'grp')  16.7 us
  transfers between devices with their start and end apart: 2, of which 1 were waited for; matrix products, arithmetic and copies ran while one was open for 3% of the time, Pallas kernels for 0%

commit v1 on v0

v1 whole, which is shorter than its diff:
```python
import jax
import jax.numpy as jnp
from jax import lax
from jax.experimental import pallas as pl
from jax.experimental.pallas import tpu as pltpu
from jax.sharding import PartitionSpec as P

F32 = jnp.float32
BF16 = jnp.bfloat16
MESH = pl.DeviceIdType.MESH

HEADS = 4
RATIO = 5
WIDTH = 128
LEN = 224
FEATURES = 2560
HALF = 1280
ROWS = 40
MEMBERS = 8
NX, NY, NZ = 4, 8, 8
EXPONENT_SCALE = 1.4426950408889634 * WIDTH ** -0.5
NT = (((1,), (1,)), ((), ()))


def softmax_columns(scores, weight):
    top = jnp.max(scores, axis=0, keepdims=True)
    grown = jnp.exp2((scores - top) * EXPONENT_SCALE)
    total = jnp.sum(grown, axis=0, keepdims=True)
    return (grown * (weight / total)).astype(BF16)


def head_gradient(keys, queries, cotangent, alive):
    upper = lax.broadcasted_iota(jnp.int32, (128, 128), 0) <= lax.broadcasted_iota(jnp.int32, (128, 128), 1)
    corner = lax.broadcasted_iota(jnp.int32, (96, 96), 0) <= lax.broadcasted_iota(jnp.int32, (96, 96), 1)
    total = None
    for h in range(RATIO):
        cols = slice(h * WIDTH, (h + 1) * WIDTH)
        early = lax.dot_general(keys[:128], queries[:128, cols], NT, preferred_element_type=F32)
        late = lax.dot_general(keys, queries[128:, cols], NT, preferred_element_type=F32)
        early = jnp.where(upper, early, -1e30)
        late = jnp.concatenate([late[:128], jnp.where(corner, late[128:], -1e30)], 0)
        early = softmax_columns(early, alive[:, :128])
        late = softmax_columns(late, alive[:, 128:])
        probs = jnp.concatenate(
            [jnp.concatenate([early, jnp.zeros((96, 128), BF16)], 0), late], 1
        )
        part = jnp.dot(probs, cotangent[:, cols], preferred_element_type=F32)
        total = part if total is None else total + part
    return total


def kernel(
    hid, queries, keys, logp, length_ref, reward_ref, w_ref,
    gw_ref, gi_ref,
    qb, kb, gb, hb, wb, ht, ub, vg, rw_src, rw,
    pb, s1s, s1r, qs, s2s, s2r, rs, s3s, s3r, zo, zs, zr, fs, fr,
    ws, wg, wf, go, gs,
    in_sem, ex_send, ex_recv, rw_send, rw_recv,
    s1_send, s1_recv, s2_send, s2_recv, s3_send, s3_recv, z_send, z_recv, f_send, f_recv,
    wz_send, wz_recv, wx_send, wx_recv, wy_send, wy_recv, go_sem, gs_send, gs_recv,
):
    g = lax.axis_index("grp")
    f = lax.axis_index("fsdp")
    c = lax.rem(g, 2)
    yh = g // 2
    yl = lax.rem(f, 2)
    x = lax.rem(f // 2, NX)
    z = f // (2 * NX)
    zc = z // 4
    zi = lax.rem(z, 4)
    y = 2 * yh + yl

    def at(z_, x_, y_, c_):
        return (2 * (y_ // 2) + c_, (z_ * NX + x_) * 2 + lax.rem(y_, 2))

    sibling = at(z, x, y, 1 - c)
    group = [(lax.rem(g + d, MEMBERS), f) for d in range(1, MEMBERS)]
    up = at(z, x, lax.rem(y + 1, NY), c)
    down = at(z, x, lax.rem(y + NY - 1, NY), c)
    xs = [at(z, lax.rem(x + d, NX), y, c) for d in range(1, NX)]
    zs_both = [at(lax.rem(z + d, NZ), x, y, k) for d in range(1, NZ) for k in range(2)]

    barrier = pltpu.get_barrier_semaphore()
    partners = group + [up, down] + xs + zs_both
    for device in partners:
        pl.semaphore_signal(barrier, inc=1, device_id=device, device_id_type=MESH)

    def remote(src, dst, send, recv, device):
        return pltpu.make_async_remote_copy(
            src_ref=src, dst_ref=dst, send_sem=send, recv_sem=recv, device_id=device, device_id_type=MESH
        )

    loads = []
    for j in range(HEADS):
        wide = pl.ds(j * RATIO * WIDTH, RATIO * WIDTH)
        loads.append([
            pltpu.make_async_copy(keys.at[:, pl.ds(j * WIDTH, WIDTH)], kb.at[j], in_sem.at[3 * j]),
            pltpu.make_async_copy(queries.at[:, wide], qb.at[j], in_sem.at[3 * j + 1]),
            pltpu.make_async_copy(logp.at[:, wide], gb.at[j], in_sem.at[3 * j + 2]),
        ])
    load_w = pltpu.make_async_copy(w_ref, wb, in_sem.at[12])
    load_h = pltpu.make_async_copy(hid.at[:, pl.ds(pl.multiple_of(c * HALF, 128), HALF)], hb.at[0], in_sem.at[13])
    for copy in loads[0] + loads[1] + [load_w] + loads[2] + loads[3] + [load_h]:
        copy.start()

    reward = reward_ref[0, 0].astype(F32)
    length = length_ref[0, 0]
    row = lax.broadcasted_iota(jnp.int32, (8, 128), 0)
    rw_src[...] = jnp.where(row == 0, reward, length.astype(F32))

    alive = jnp.where(lax.broadcasted_iota(jnp.int32, (1, LEN), 1) < length, 1.0, 0.0).astype(F32)
    for j in range(HEADS):
        for copy in loads[j]:
            copy.wait()
        ub[0, j] = head_gradient(kb[j], qb[j], gb[j], alive).astype(BF16)

    load_w.wait()
    shard = wb[...].astype(F32)
    ws[...] = jnp.concatenate([shard[:, p * 128:(p + 1) * 128] for p in range(4)], 0).astype(BF16)

    @pl.when(c == zc)
    def _():
        wg[yl, x, zi] = ws[...]

    load_h.wait()
    for b in range(10):
        cols = slice(b * 128, (b + 1) * 128)
        ht[0, cols, :] = hb[0, :, cols].T

    pl.semaphore_wait(barrier, len(partners))

    reward_copies = [remote(rw_src, rw.at[d], rw_send.at[d], rw_recv.at[d], group[d - 1]) for d in range(1, MEMBERS)]
    for copy in reward_copies:
        copy.start()
    share_u = remote(ub.at[0], ub.at[1], ex_send.at[0], ex_recv.at[0], sibling)
    share_h = remote(
        hid.at[:, pl.ds(pl.multiple_of((1 - c) * HALF, 128), HALF)], hb.at[1], ex_send.at[1], ex_recv.at[1], sibling
    )
    share_h.start()
    share_u.start()

    def w_send(i):
        other = 4 * c + i
        return remote(ws, wg.at[yl, x, zi], wz_send.at[i], wz_recv.at[zi], at(other, x, y, zc))

    def w_arrival(i):
        return remote(ws, wg.at[yl, x, i], wz_send.at[i], wz_recv.at[i], at(4 * c + i, x, y, zc))

    for i in range(4):
        @pl.when(4 * c + i != z)
        def _(i=i):
            w_send(i).start()

    share_h.wait_recv()
    for b in range(10):
        cols = slice(b * 128, (b + 1) * 128)
        ht[1, cols, :] = hb[1, :, cols].T
    share_u.wait_recv()

    for copy in reward_copies:
        copy.wait_recv()
    rw[0] = rw_src[...]
    everyone = rw[...]
    rewards = everyone[:, 0:1, :]
    average = jnp.sum(rewards, axis=0) / MEMBERS
    second = jnp.sum(rewards * rewards, axis=0) / MEMBERS
    spread = jnp.maximum(jnp.sqrt(second - average * average), 1.0)

    def factor_of(rows):
        return -((rows[0:1] - average) / spread) / (MEMBERS * rows[1:2])

    own_factor = factor_of(rw_src[...])
    other_factor = factor_of(rw[7 - 6 * c])

    s1 = []
    for j in range(HEADS):
        lanes = slice(j * 128, (j + 1) * 128)
        vg[0, :, lanes] = (ub[0, j].astype(F32) * own_factor).astype(BF16)
        vg[1, :, lanes] = (ub[1, j].astype(F32) * other_factor).astype(BF16)
        for b in range(4):
            rows = slice(b * 320, (b + 1) * 320)
            part = jnp.dot(ht[0, rows, :], vg[0, :, lanes], preferred_element_type=F32)
            part += jnp.dot(ht[1, rows, :], vg[1, :, lanes], preferred_element_type=F32)
            pb[j, b * 4:(b + 1) * 4] = part.reshape(4, 2, ROWS, 128)
        s1s[j] = pb[j, :, 1 - yl].reshape(640, 128).astype(BF16)
        copies = [
            remote(s1s.at[j, pl.ds(0, 320)], s1r.at[j, pl.ds(0, 320)], s1_send.at[j, 0], s1_recv.at[j, 0], up),
            remote(s1s.at[j, pl.ds(320, 320)], s1r.at[j, pl.ds(320, 320)], s1_send.at[j, 1], s1_recv.at[j, 1], down),
        ]
        for copy in copies:
            copy.start()
        s1.append(copies)

    for i in range(4):
        @pl.when(4 * c + i != z)
        def _(i=i):
            w_arrival(i).wait_recv()
    wx = [remote(wg.at[yl, x], wg.at[yl, x], wx_send.at[d], wx_recv.at[d], xs[d]) for d in range(NX - 1)]
    for copy in wx:
        copy.start()

    s2 = []
    for j in range(HEADS):
        for copy in s1[j]:
            copy.wait_recv()
        qs[j] = (pb[j, :, yl] + s1r[j].astype(F32).reshape(16, ROWS, 128)).reshape(4, 4, ROWS, 128)
        copies = []
        for d in range(NX - 1):
            s2s[j, d] = qs[j, :, lax.rem(x + d + 1, NX)].reshape(160, 128).astype(BF16)
            copies.append(remote(s2s.at[j, d], s2r.at[j, d], s2_send.at[j, d], s2_recv.at[j, d], xs[d]))
            copies[-1].start()
        s2.append(copies)

    def wx_arrival(d):
        return remote(
            wg.at[yl, x], wg.at[yl, lax.rem(x + NX - 1 - d, NX)], wx_send.at[d], wx_recv.at[d], xs[d]
        )

    for d in range(NX - 1):
        wx_arrival(d).wait_recv()
    wy = [
        remote(wg.at[yl, pl.ds(0, 2)], wg.at[yl, pl.ds(0, 2)], wy_send.at[0], wy_recv.at[0], up),
        remote(wg.at[yl, pl.ds(2, 2)], wg.at[yl, pl.ds(2, 2)], wy_send.at[1], wy_recv.at[1], down),
    ]
    for copy in wy:
        copy.start()

    def s3_copy(j):
        slot = lax.rem(j - yh + 4, 4)
        return remote(s3s.at[j], s3r.at[slot], s3_send.at[j], s3_recv.at[slot], at(z, x, 2 * j + yl, c))

    for j in range(HEADS):
        for copy in s2[j]:
            copy.wait_recv()
        total = qs[j, :, x].reshape(160, 128)
        for d in range(NX - 1):
            total += s2r[j, d].astype(F32)
        rs[j] = total
        s3s[j] = total.astype(BF16)

        @pl.when(j != yh)
        def _(j=j):
            s3_copy(j).start()

    for slot in range(1, 4):
        remote(s3s.at[0], s3r.at[slot], s3_send.at[0], s3_recv.at[slot], sibling).wait_recv()
    total = rs[yh]
    for slot in range(1, 4):
        total += s3r[slot].astype(F32)
    total = total.reshape(4, ROWS, 128)
    zo[...] = total
    zs[...] = jnp.concatenate([total, jnp.zeros((4, 8, 128), F32)], 1).astype(BF16)

    def z_copy(i):
        other = 4 * c + i
        slot = lax.rem(other - z + NZ, NZ)
        return remote(zs.at[i], zr.at[slot], z_send.at[i], z_recv.at[slot], at(other, x, y, c))

    for i in range(4):
        @pl.when(4 * c + i != z)
        def _(i=i):
            z_copy(i).start()

    remote(wg.at[yl, pl.ds(0, 2)], wg.at[1 - yl, pl.ds(0, 2)], wy_send.at[0], wy_recv.at[0], up).wait_recv()
    remote(wg.at[yl, pl.ds(2, 2)], wg.at[1 - yl, pl.ds(2, 2)], wy_send.at[1], wy_recv.at[1], down).wait_recv()
    for b in range(16):
        even = wg[0, b % 4, b // 4].astype(F32)
        odd = wg[1, b % 4, b // 4].astype(F32)
        for p in range(4):
            part = slice(p * ROWS, (p + 1) * ROWS)
            wf[b * 80:(b + 1) * 80, p * 128:(p + 1) * 128] = jnp.concatenate([even[part], odd[part]], 0).astype(BF16)
    for b in range(5):
        cols = slice(b * 256, (b + 1) * 256)
        gs[:, cols] = lax.dot_general(vg[1], wf[cols, :], NT, preferred_element_type=F32).astype(BF16)
    mine = gi_ref.at[:, pl.ds(pl.multiple_of(c * HALF, 128), HALF)]
    theirs = gi_ref.at[:, pl.ds(pl.multiple_of((1 - c) * HALF, 128), HALF)]
    give = remote(gs, mine, gs_send, gs_recv, sibling)
    take = remote(gs, theirs, gs_send, gs_recv, sibling)
    give.start()
    for b in range(5):
        cols = slice(b * 256, (b + 1) * 256)
        go[:, cols] = lax.dot_general(vg[0], wf[cols, :], NT, preferred_element_type=F32).astype(BF16)
    keep = pltpu.make_async_copy(go, mine, go_sem)
    keep.start()

    share = remote(fs, fr, f_send, f_recv, sibling)

    @pl.when(c == zc)
    def _():
        for slot in range(1, NZ):
            remote(zs.at[0], zr.at[slot], z_send.at[0], z_recv.at[slot], sibling).wait_recv()
        total = zo[zi]
        for slot in range(1, NZ):
            total += zr[slot].astype(F32)[:ROWS]
        turned = pltpu.roll(total, 64, 1)
        fs[...] = jnp.where(c == 0, turned, total)
        share.start()
        gw_ref[...] = jnp.where(c == 0, total, turned)[:, :64]
        share.wait_send()

    @pl.when(c != zc)
    def _():
        share.wait_recv()
        gw_ref[...] = fr[:, :64]

    for copy in reward_copies + [share_u, share_h] + wx + wy:
        copy.wait_send()
    for copies in s1 + s2:
        for copy in copies:
            copy.wait_send()
    for i in range(4):
        @pl.when(4 * c + i != z)
        def _(i=i):
            w_send(i).wait_send()
            z_copy(i).wait_send()

        @pl.when(i != yh)
        def _(i=i):
            s3_copy(i).wait_send()
    keep.wait()
    give.wait_send()
    take.wait_recv()


def local(hidden_in, queries, keys, logp_grad, lengths, rewards, w_value):
    vmem = pltpu.VMEM
    dma = pltpu.SemaphoreType.DMA
    anywhere = pl.BlockSpec(memory_space=pl.ANY)
    scalar = pl.BlockSpec(memory_space=pltpu.SMEM)
    gradient, input_grad = pl.pallas_call(
        kernel,
        out_shape=(
            jax.ShapeDtypeStruct((ROWS, 64), F32),
            jax.ShapeDtypeStruct((LEN, FEATURES), BF16),
        ),
        in_specs=[anywhere] * 4 + [scalar] * 2 + [anywhere],
        out_specs=(pl.BlockSpec(memory_space=pltpu.VMEM), anywhere),
        scratch_shapes=[
            vmem((HEADS, LEN, RATIO * WIDTH), BF16),
            vmem((HEADS, LEN, WIDTH), BF16),
            vmem((HEADS, LEN, RATIO * WIDTH), BF16),
            vmem((2, LEN, HALF), BF16),
            vmem((ROWS, 512), BF16),
            vmem((2, HALF, LEN), BF16),
            vmem((2, HEADS, LEN, WIDTH), BF16),
            vmem((2, LEN, 512), BF16),
            vmem((8, 128), F32),
            vmem((MEMBERS, 8, 128), F32),
            vmem((HEADS, 16, 2, ROWS, 128), F32),
            vmem((HEADS, 640, 128), BF16),
            vmem((HEADS, 640, 128), BF16),
            vmem((HEADS, 4, NX, ROWS, 128), F32),
            vmem((HEADS, 3, 160, 128), BF16),
            vmem((HEADS, 3, 160, 128), BF16),
            vmem((HEADS, 160, 128), F32),
            vmem((HEADS, 160, 128), BF16),
            vmem((4, 160, 128), BF16),
            vmem((4, ROWS, 128), F32),
            vmem((4, 48, 128), BF16),
            vmem((NZ, 48, 128), BF16),
            vmem((ROWS, 128), F32),
            vmem((ROWS, 128), F32),
            vmem((160, 128), BF16),
            vmem((2, NX, 4, 160, 128), BF16),
            vmem((HALF, 512), BF16),
            vmem((LEN, HALF), BF16),
            vmem((LEN, HALF), BF16),
            dma((14,)),
            dma((2,)), dma((2,)),
            dma((MEMBERS,)), dma((MEMBERS,)),
            dma((HEADS, 2)), dma((HEADS, 2)),
            dma((HEADS, 3)), dma((HEADS, 3)),
            dma((HEADS,)), dma((4,)),
            dma((4,)), dma((NZ,)),
            dma, dma,
            dma((4,)), dma((4,)),
            dma((3,)), dma((3,)),
            dma((2,)), dma((2,)),
            dma, dma, dma,
        ],
        compiler_params=pltpu.CompilerParams(
            collective_id=0, has_side_effects=True, vmem_limit_bytes=56 * 2 ** 20
        ),
    )(
        hidden_in.reshape(LEN, FEATURES), queries.reshape(LEN, FEATURES), keys.reshape(LEN, 512),
        logp_grad.reshape(LEN, FEATURES), lengths, rewards, w_value,
    )
    return gradient, input_grad.reshape(1, 1, LEN, FEATURES)


def solution(mesh):
    placed = (
        P("fsdp", "grp", None, None),
        P("fsdp", "grp", None, None),
        P("fsdp", "grp", None, None),
        P("fsdp", "grp", None, None),
        P("fsdp", "grp"),
        P("fsdp", "grp"),
        P("fsdp", None),
    )
    return jax.shard_map(
        local,
        mesh=mesh,
        in_specs=placed,
        out_specs=(P("fsdp", "grp"), P("fsdp", "grp", None, None)),
        check_vma=False,
    )
```

time: 657 us -> 58.9 us (0.09)
  the two profiles are of different devices: /device:TPU:16 before, /device:TPU:1 now
where the time goes in v1:
time: 58.9 us; the launch traced here: 58.6 us
  Pallas kernels  53 us (90%)
  local copies, waits for them, and re-layouts  3.67 us (6%)
  between operations  1.93 us (3%)
    pallas_call x1, Pallas kernels, local(): pl.pallas_call(kernel, out_shape=(jax.ShapeDtypeStruct((ROWS, 64), F32),...  53 us
    unnamed x2, local copies, waits for them, and re-layouts  3.67 us

profile of v1, /device:TPU:1, one launch (start us, length us, event | category | flops | bytes accessed | tf_op | source)
XLA Modules:
  0.0 58.6 jit_solution(10060662610435980914)
XLA Ops:
  1.9 53.0 %shard_map.86 = (f32[40,64]{1,0:T(8,128)}, bf16[224,2560]{1,0:T(8,128)(2,1)}) custom-call(bf16[224,2560]{1,0:T(8,128)(2,1)} %bitcast.6, bf16[224,2560]{1,0:T(8,128)(2,1)} %bitcast.7, bf16[224,512]{1,0:T(8,128)(2,1)} %bitcast.9, bf16[224,2560]{1,0:T(8,128)(2,1)} %bitcast.8, s32[1,1]{1,0:T(1,128)S(6)} %copy.11.length_ref, s32[1,1]{1,0:T(1,128)S(6)} %copy.12.reward_ref, ...), custom_call_target="tpu_custom_call" | custom-call | tf_op jit(solution)/shard_map/pallas_call | solution.py:330
  54.9 1.3 %copy.13 = f32[40,64]{1,0:T(8,128)} copy(f32[40,64]{1,0:T(8,128)} %get-tuple-element.8) | data formatting | bytes 20480
  56.3 2.3 %copy.14 = bf16[1,1,224,2560]{3,2,1,0:T(8,128)(2,1)} copy(bf16[1,1,224,2560]{3,2,1,0:T(8,128)(2,1)} %bitcast.5) | data formatting | bytes 2293760

commit v2 on v1

--- a/solution.py
+++ b/solution.py
@@ -18,6 +18,7 @@
 ROWS = 40
 MEMBERS = 8
 NX, NY, NZ = 4, 8, 8
+SPLIT = 112
 EXPONENT_SCALE = 1.4426950408889634 * WIDTH ** -0.5
 NT = (((1,), (1,)), ((), ()))
 
@@ -54,10 +55,11 @@
     gw_ref, gi_ref,
     qb, kb, gb, hb, wb, ht, ub, vg, rw_src, rw,
     pb, s1s, s1r, qs, s2s, s2r, rs, s3s, s3r, zo, zs, zr, fs, fr,
-    ws, wg, wf, go, gs,
+    ws, wg, wf, gs,
     in_sem, ex_send, ex_recv, rw_send, rw_recv,
     s1_send, s1_recv, s2_send, s2_recv, s3_send, s3_recv, z_send, z_recv, f_send, f_recv,
-    wz_send, wz_recv, wx_send, wx_recv, wy_send, wy_recv, go_sem, gs_send, gs_recv,
+    wz_send, wz_recv, wx_send, wx_recv, wy_send, wy_recv,
+    ry_send, ry_recv, rx_send, rx_recv, rz_send, rz_recv, gs_send, gs_recv,
 ):
     g = lax.axis_index("grp")
     f = lax.axis_index("fsdp")
@@ -109,7 +111,8 @@
     rw_src[...] = jnp.where(row == 0, reward, length.astype(F32))
 
     alive = jnp.where(lax.broadcasted_iota(jnp.int32, (1, LEN), 1) < length, 1.0, 0.0).astype(F32)
-    for j in range(HEADS):
+
+    def attend(j):
         for copy in loads[j]:
             copy.wait()
         ub[0, j] = head_gradient(kb[j], qb[j], gb[j], alive).astype(BF16)
@@ -121,41 +124,87 @@
     @pl.when(c == zc)
     def _():
         wg[yl, x, zi] = ws[...]
+
+    attend(0)
+
+    pl.semaphore_wait(barrier, len(partners))
+
+    reward_copies = [remote(rw_src, rw.at[d], rw_send.at[d], rw_recv.at[d], group[d - 1]) for d in range(1, MEMBERS)]
+    for copy in reward_copies:
+        copy.start()
+    share_h = remote(
+        hid.at[:, pl.ds(pl.multiple_of((1 - c) * HALF, 128), HALF)], hb.at[1], ex_send.at[HEADS], ex_recv.at[HEADS], sibling
+    )
+    share_h.start()
+    share_u = [remote(ub.at[0, j], ub.at[1, j], ex_send.at[j], ex_recv.at[j], sibling) for j in range(HEADS)]
+    share_u[0].start()
+
+    first, rest = pl.ds(0, SPLIT), pl.ds(SPLIT, 160 - SPLIT)
+
+    def w_send(i):
+        other = 4 * c + i
+        return remote(ws.at[first], wg.at[yl, x, zi, first], wz_send.at[i], wz_recv.at[zi], at(other, x, y, zc))
+
+    def w_arrival(i):
+        return remote(
+            ws.at[first], wg.at[yl, x, i, first], wz_send.at[i], wz_recv.at[i], at(4 * c + i, x, y, zc)
+        )
+
+    for i in range(4):
+        @pl.when(4 * c + i != z)
+        def _(i=i):
+            w_send(i).start()
+
+    rest_y = remote(ws.at[rest], wg.at[yl, x, zi, rest], ry_send, ry_recv, up)
+    rest_y_arrival = remote(ws.at[rest], wg.at[1 - yl, x, zi, rest], ry_send, ry_recv, up)
+    rest_x = [
+        remote(wg.at[:, x, zi, rest], wg.at[:, x, zi, rest], rx_send.at[d], rx_recv.at[d], xs[d]) for d in range(NX - 1)
+    ]
+    rest_x_arrival = [
+        remote(
+            wg.at[:, x, zi, rest], wg.at[:, lax.rem(x + NX - 1 - d, NX), zi, rest],
+            rx_send.at[d], rx_recv.at[d], xs[d],
+        )
+        for d in range(NX - 1)
+    ]
+    rest_z = [
+        remote(
+            wg.at[:, :, zi, rest], wg.at[:, :, zi, rest], rz_send.at[d], rz_recv.at[zi],
+            at(lax.rem(z + d + 1, NZ), x, y, c),
+        )
+        for d in range(NZ - 1)
+    ]
+
+    def rest_z_arrival(i):
+        return remote(
+            wg.at[:, :, i, rest], wg.at[:, :, i, rest], rz_send.at[0], rz_recv.at[i], at(4 * c + i, x, y, c)
+        )
+
+    @pl.when(c == zc)
+    def _():
+        rest_y.start()
+
+    for j in range(1, HEADS):
+        attend(j)
+        share_u[j].start()
 
     load_h.wait()
     for b in range(10):
         cols = slice(b * 128, (b + 1) * 128)
         ht[0, cols, :] = hb[0, :, cols].T
 
-    pl.semaphore_wait(barrier, len(partners))
-
-    reward_copies = [remote(rw_src, rw.at[d], rw_send.at[d], rw_recv.at[d], group[d - 1]) for d in range(1, MEMBERS)]
-    for copy in reward_copies:
-        copy.start()
-    share_u = remote(ub.at[0], ub.at[1], ex_send.at[0], ex_recv.at[0], sibling)
-    share_h = remote(
-        hid.at[:, pl.ds(pl.multiple_of((1 - c) * HALF, 128), HALF)], hb.at[1], ex_send.at[1], ex_recv.at[1], sibling
-    )
-    share_h.start()
-    share_u.start()
-
-    def w_send(i):
-        other = 4 * c + i
-        return remote(ws, wg.at[yl, x, zi], wz_send.at[i], wz_recv.at[zi], at(other, x, y, zc))
-
-    def w_arrival(i):
-        return remote(ws, wg.at[yl, x, i], wz_send.at[i], wz_recv.at[i], at(4 * c + i, x, y, zc))
-
-    for i in range(4):
-        @pl.when(4 * c + i != z)
-        def _(i=i):
-            w_send(i).start()
+    @pl.when(c == zc)
+    def _():
+        rest_y_arrival.wait_recv()
+        for copy in rest_x:
+            copy.start()
 
     share_h.wait_recv()
     for b in range(10):
         cols = slice(b * 128, (b + 1) * 128)
         ht[1, cols, :] = hb[1, :, cols].T
-    share_u.wait_recv()
+    for copy in share_u:
+        copy.wait_recv()
 
     for copy in reward_copies:
         copy.wait_recv()
@@ -191,11 +240,19 @@
             copy.start()
         s1.append(copies)
 
+    @pl.when(c == zc)
+    def _():
+        for copy in rest_x_arrival:
+            copy.wait_recv()
+        for copy in rest_z:
+            copy.start()
+
     for i in range(4):
         @pl.when(4 * c + i != z)
         def _(i=i):
             w_arrival(i).wait_recv()
-    wx = [remote(wg.at[yl, x], wg.at[yl, x], wx_send.at[d], wx_recv.at[d], xs[d]) for d in range(NX - 1)]
+    ours = wg.at[yl, x, :, first]
+    wx = [remote(ours, ours, wx_send.at[d], wx_recv.at[d], xs[d]) for d in range(NX - 1)]
     for copy in wx:
         copy.start()
 
@@ -213,14 +270,19 @@
 
     def wx_arrival(d):
         return remote(
-            wg.at[yl, x], wg.at[yl, lax.rem(x + NX - 1 - d, NX)], wx_send.at[d], wx_recv.at[d], xs[d]
+            ours, wg.at[yl, lax.rem(x + NX - 1 - d, NX), :, first], wx_send.at[d], wx_recv.at[d], xs[d]
         )
 
     for d in range(NX - 1):
         wx_arrival(d).wait_recv()
+    lower, upper = pl.ds(0, 2), pl.ds(2, 2)
     wy = [
-        remote(wg.at[yl, pl.ds(0, 2)], wg.at[yl, pl.ds(0, 2)], wy_send.at[0], wy_recv.at[0], up),
-        remote(wg.at[yl, pl.ds(2, 2)], wg.at[yl, pl.ds(2, 2)], wy_send.at[1], wy_recv.at[1], down),
+        remote(wg.at[yl, lower, :, first], wg.at[yl, lower, :, first], wy_send.at[0], wy_recv.at[0], up),
+        remote(wg.at[yl, upper, :, first], wg.at[yl, upper, :, first], wy_send.at[1], wy_recv.at[1], down),
+    ]
+    wy_arrival = [
+        remote(wg.at[yl, lower, :, first], wg.at[1 - yl, lower, :, first], wy_send.at[0], wy_recv.at[0], up),
+        remote(wg.at[yl, upper, :, first], wg.at[1 - yl, upper, :, first], wy_send.at[1], wy_recv.at[1], down),
     ]
     for copy in wy:
         copy.start()
@@ -261,8 +323,12 @@
         def _(i=i):
             z_copy(i).start()
 
-    remote(wg.at[yl, pl.ds(0, 2)], wg.at[1 - yl, pl.ds(0, 2)], wy_send.at[0], wy_recv.at[0], up).wait_recv()
-    remote(wg.at[yl, pl.ds(2, 2)], wg.at[1 - yl, pl.ds(2, 2)], wy_send.at[1], wy_recv.at[1], down).wait_recv()
+    for copy in wy_arrival:
+        copy.wait_recv()
+    for i in range(4):
+        @pl.when(4 * c + i != z)
+        def _(i=i):
+            rest_z_arrival(i).wait_recv()
     for b in range(16):
         even = wg[0, b % 4, b // 4].astype(F32)
         odd = wg[1, b % 4, b // 4].astype(F32)
@@ -272,16 +338,36 @@
     for b in range(5):
         cols = slice(b * 256, (b + 1) * 256)
         gs[:, cols] = lax.dot_general(vg[1], wf[cols, :], NT, preferred_element_type=F32).astype(BF16)
-    mine = gi_ref.at[:, pl.ds(pl.multiple_of(c * HALF, 128), HALF)]
-    theirs = gi_ref.at[:, pl.ds(pl.multiple_of((1 - c) * HALF, 128), HALF)]
-    give = remote(gs, mine, gs_send, gs_recv, sibling)
-    take = remote(gs, theirs, gs_send, gs_recv, sibling)
+    give = remote(gs, gi_ref.at[c], gs_send, gs_recv, sibling)
+    take = remote(gs, gi_ref.at[1 - c], gs_send, gs_recv, sibling)
     give.start()
     for b in range(5):
         cols = slice(b * 256, (b + 1) * 256)
-        go[:, cols] = lax.dot_general(vg[0], wf[cols, :], NT, preferred_element_type=F32).astype(BF16)
-    keep = pltpu.make_async_copy(go, mine, go_sem)
-    keep.start()
+        gi_ref[c, :, cols] = lax.dot_general(vg[0], wf[cols, :], NT, preferred_element_type=F32).astype(BF16)
+
+    for copy in reward_copies + share_u + [share_h] + wx + wy:
+        copy.wait_send()
+    for copies in s1 + s2:
+        for copy in copies:
+            copy.wait_send()
+
+    @pl.when(c == zc)
+    def _():
+        rest_y.wait_send()
+        for copy in rest_x + rest_z:
+            copy.wait_send()
+
+    for i in range(4):
+        @pl.when(4 * c + i != z)
+        def _(i=i):
+            w_send(i).wait_send()
+            z_copy(i).wait_send()
+
+        @pl.when(i != yh)
+        def _(i=i):
+            s3_copy(i).wait_send()
+    give.wait_send()
+    take.wait_recv()
 
     share = remote(fs, fr, f_send, f_recv, sibling)
 
@@ -303,23 +389,15 @@
         share.wait_recv()
         gw_ref[...] = fr[:, :64]
 
-    for copy in reward_copies + [share_u, share_h] + wx + wy:
-        copy.wait_send()
-    for copies in s1 + s2:
-        for copy in copies:
-            copy.wait_send()
-    for i in range(4):
-        @pl.when(4 * c + i != z)
-        def _(i=i):
-            w_send(i).wait_send()
-            z_copy(i).wait_send()
-
-        @pl.when(i != yh)
-        def _(i=i):
-            s3_copy(i).wait_send()
-    keep.wait()
-    give.wait_send()
-    take.wait_recv()
+
+def store(gradient, halves, gradient_out, input_out, sem):
+    copies = [pltpu.make_async_copy(gradient, gradient_out, sem.at[2])]
+    for k in range(2):
+        copies.append(pltpu.make_async_copy(halves.at[k], input_out.at[:, pl.ds(k * HALF, HALF)], sem.at[k]))
+    for copy in copies:
+        copy.start()
+    for copy in copies:
+        copy.wait()
 
 
 def local(hidden_in, queries, keys, logp_grad, lengths, rewards, w_value):
@@ -327,14 +405,14 @@
     dma = pltpu.SemaphoreType.DMA
     anywhere = pl.BlockSpec(memory_space=pl.ANY)
     scalar = pl.BlockSpec(memory_space=pltpu.SMEM)
-    gradient, input_grad = pl.pallas_call(
+    gradient, halves = pl.pallas_call(
         kernel,
         out_shape=(
-            jax.ShapeDtypeStruct((ROWS, 64), F32),
-            jax.ShapeDtypeStruct((LEN, FEATURES), BF16),
+            vmem((ROWS, 64), F32),
+            vmem((2, LEN, HALF), BF16),
         ),
         in_specs=[anywhere] * 4 + [scalar] * 2 + [anywhere],
-        out_specs=(pl.BlockSpec(memory_space=pltpu.VMEM), anywhere),
+        out_specs=(pl.BlockSpec(memory_space=pltpu.VMEM),) * 2,
         scratch_shapes=[
             vmem((HEADS, LEN, RATIO * WIDTH), BF16),
             vmem((HEADS, LEN, WIDTH), BF16),
@@ -364,9 +442,8 @@
             vmem((2, NX, 4, 160, 128), BF16),
             vmem((HALF, 512), BF16),
             vmem((LEN, HALF), BF16),
-            vmem((LEN, HALF), BF16),
             dma((14,)),
-            dma((2,)), dma((2,)),
+            dma((HEADS + 1,)), dma((HEADS + 1,)),
             dma((MEMBERS,)), dma((MEMBERS,)),
             dma((HEADS, 2)), dma((HEADS, 2)),
             dma((HEADS, 3)), dma((HEADS, 3)),
@@ -376,7 +453,8 @@
             dma((4,)), dma((4,)),
             dma((3,)), dma((3,)),
             dma((2,)), dma((2,)),
-            dma, dma, dma,
+            dma, dma, dma((3,)), dma((3,)), dma((NZ,)), dma((4,)),
+            dma, dma,
         ],
         compiler_params=pltpu.CompilerParams(
             collective_id=0, has_side_effects=True, vmem_limit_bytes=56 * 2 ** 20
@@ -385,6 +463,17 @@
         hidden_in.reshape(LEN, FEATURES), queries.reshape(LEN, FEATURES), keys.reshape(LEN, 512),
         logp_grad.reshape(LEN, FEATURES), lengths, rewards, w_value,
     )
+    gradient, input_grad = pl.pallas_call(
+        store,
+        out_shape=(
+            jax.ShapeDtypeStruct((ROWS, 64), F32),
+            jax.ShapeDtypeStruct((LEN, FEATURES), BF16),
+        ),
+        in_specs=[pl.BlockSpec(memory_space=pltpu.VMEM)] * 2,
+        out_specs=(anywhere,) * 2,
+        scratch_shapes=[dma((3,))],
+        compiler_params=pltpu.CompilerParams(vmem_limit_bytes=4 * 2 ** 20),
+    )(gradient, halves)
     return gradient, input_grad.reshape(1, 1, LEN, FEATURES)
 
 

time: 58.9 us -> 50.1 us (0.85)
  Pallas kernels: 53 us -> 48 us
  local copies, waits for them, and re-layouts: 3.67 us -> 0 us
    pallas_call x1 -> x2, Pallas kernels: 53 us -> 48 us  [the longest x1 47 us: local(): pl.pallas_call(kernel, out_shape=(vmem((ROWS, 64), F32), vmem((2, LEN, HA...]
    unnamed x2 -> x0, local copies, waits for them, and re-layouts: 3.67 us -> none
where the time goes in v2:
time: 50.1 us; the launch traced here: 49.9 us
  Pallas kernels  48 us (96%)
  between operations  1.93 us (4%)
    pallas_call x1, Pallas kernels, local(): pl.pallas_call(kernel, out_shape=(vmem((ROWS, 64), F32), vmem((2, LEN, HA...  47 us
    pallas_call x1, Pallas kernels, local(): pl.pallas_call(store, out_shape=(jax.ShapeDtypeStruct((ROWS, 64), F32), j...  1.03 us

profile of v2, /device:TPU:1, one launch (start us, length us, event | category | flops | bytes accessed | tf_op | source)
XLA Modules:
  0.0 49.9 jit_solution(8908379789113665520)
XLA Ops:
  1.9 47.0 %shard_map.86 = (f32[40,64]{1,0:T(8,128)S(1)}, bf16[2,224,1280]{2,1,0:T(8,128)(2,1)S(1)}) custom-call(bf16[224,2560]{1,0:T(8,128)(2,1)} %bitcast.5, bf16[224,2560]{1,0:T(8,128)(2,1)} %bitcast.6, bf16[224,512]{1,0:T(8,128)(2,1)} %bitcast.8, bf16[224,2560]{1,0:T(8,128)(2,1)} %bitcast.7, s32[1,1]{1,0:T(1,128)S(6)} %copy.9.length_ref, ...), custom_call_target="tpu_custom_call" | custom-call | tf_op jit(solution)/shard_map/pallas_call | solution.py:408
  48.9 1.0 %shard_map.87 = (f32[40,64]{1,0:T(8,128)}, bf16[224,2560]{1,0:T(8,128)(2,1)}) custom-call(f32[40,64]{1,0:T(8,128)S(1)} %get-tuple-element.6.gradient, bf16[2,224,1280]{2,1,0:T(8,128)(2,1)S(1)} %get-tuple-element.7.halves), custom_call_target="tpu_custom_call" | custom-call | tf_op jit(solution)/shard_map/pallas_call | solution.py:466

commit v3 on v2

--- a/solution.py
+++ b/solution.py
@@ -18,7 +18,7 @@
 ROWS = 40
 MEMBERS = 8
 NX, NY, NZ = 4, 8, 8
-SPLIT = 112
+SPLIT = 96
 EXPONENT_SCALE = 1.4426950408889634 * WIDTH ** -0.5
 NT = (((1,), (1,)), ((), ()))
 
@@ -54,10 +54,10 @@
     hid, queries, keys, logp, length_ref, reward_ref, w_ref,
     gw_ref, gi_ref,
     qb, kb, gb, hb, wb, ht, ub, vg, rw_src, rw,
-    pb, s1s, s1r, qs, s2s, s2r, rs, s3s, s3r, zo, zs, zr, fs, fr,
+    pb, s1s, s1r, qs, s2s, s2r, zo, zs, zr, fs, fr,
     ws, wg, wf, gs,
     in_sem, ex_send, ex_recv, rw_send, rw_recv,
-    s1_send, s1_recv, s2_send, s2_recv, s3_send, s3_recv, z_send, z_recv, f_send, f_recv,
+    s1_send, s1_recv, s2_send, s2_recv, z_send, z_recv, f_send, f_recv,
     wz_send, wz_recv, wx_send, wx_recv, wy_send, wy_recv,
     ry_send, ry_recv, rx_send, rx_recv, rz_send, rz_recv, gs_send, gs_recv,
 ):
@@ -87,6 +87,13 @@
     for device in partners:
         pl.semaphore_signal(barrier, inc=1, device_id=device, device_id_type=MESH)
 
+    @pl.when(c == zc)
+    def _():
+        for d in range(1, NZ):
+            for e in range(1, 4):
+                sender = at(lax.rem(z + d, NZ), x, lax.rem(y + 2 * e, NY), c)
+                pl.semaphore_signal(barrier, inc=1, device_id=sender, device_id_type=MESH)
+
     def remote(src, dst, send, recv, device):
         return pltpu.make_async_remote_copy(
             src_ref=src, dst_ref=dst, send_sem=send, recv_sem=recv, device_id=device, device_id_type=MESH
@@ -127,7 +134,7 @@
 
     attend(0)
 
-    pl.semaphore_wait(barrier, len(partners))
+    pl.semaphore_wait(barrier, len(partners) + jnp.where(c == zc, 9, 12))
 
     reward_copies = [remote(rw_src, rw.at[d], rw_send.at[d], rw_recv.at[d], group[d - 1]) for d in range(1, MEMBERS)]
     for copy in reward_copies:
@@ -287,9 +294,14 @@
     for copy in wy:
         copy.start()
 
-    def s3_copy(j):
-        slot = lax.rem(j - yh + 4, 4)
-        return remote(s3s.at[j], s3r.at[slot], s3_send.at[j], s3_recv.at[slot], at(z, x, 2 * j + yl, c))
+    def z_slot(j, i):
+        return lax.rem(4 * c + i - z + NZ, NZ) * 4 + lax.rem(j - yh + 4, 4)
+
+    def z_copy(j, i):
+        slot = z_slot(j, i)
+        return remote(
+            zs.at[j, i], zr.at[slot], z_send.at[j, i], z_recv.at[slot], at(4 * c + i, x, 2 * j + yl, c)
+        )
 
     for j in range(HEADS):
         for copy in s2[j]:
@@ -297,31 +309,13 @@
         total = qs[j, :, x].reshape(160, 128)
         for d in range(NX - 1):
             total += s2r[j, d].astype(F32)
-        rs[j] = total
-        s3s[j] = total.astype(BF16)
-
-        @pl.when(j != yh)
-        def _(j=j):
-            s3_copy(j).start()
-
-    for slot in range(1, 4):
-        remote(s3s.at[0], s3r.at[slot], s3_send.at[0], s3_recv.at[slot], sibling).wait_recv()
-    total = rs[yh]
-    for slot in range(1, 4):
-        total += s3r[slot].astype(F32)
-    total = total.reshape(4, ROWS, 128)
-    zo[...] = total
-    zs[...] = jnp.concatenate([total, jnp.zeros((4, 8, 128), F32)], 1).astype(BF16)
-
-    def z_copy(i):
-        other = 4 * c + i
-        slot = lax.rem(other - z + NZ, NZ)
-        return remote(zs.at[i], zr.at[slot], z_send.at[i], z_recv.at[slot], at(other, x, y, c))
-
-    for i in range(4):
-        @pl.when(4 * c + i != z)
-        def _(i=i):
-            z_copy(i).start()
+        total = total.reshape(4, ROWS, 128)
+        zo[j] = total
+        zs[j] = jnp.concatenate([total, jnp.zeros((4, 8, 128), F32)], 1).astype(BF16)
+        for i in range(4):
+            @pl.when(z_slot(j, i) != 0)
+            def _(j=j, i=i):
+                z_copy(j, i).start()
 
     for copy in wy_arrival:
         copy.wait_recv()
@@ -361,11 +355,11 @@
         @pl.when(4 * c + i != z)
         def _(i=i):
             w_send(i).wait_send()
-            z_copy(i).wait_send()
-
-        @pl.when(i != yh)
-        def _(i=i):
-            s3_copy(i).wait_send()
+
+        for j in range(HEADS):
+            @pl.when(z_slot(j, i) != 0)
+            def _(i=i, j=j):
+                z_copy(j, i).wait_send()
     give.wait_send()
     take.wait_recv()
 
@@ -373,10 +367,10 @@
 
     @pl.when(c == zc)
     def _():
-        for slot in range(1, NZ):
-            remote(zs.at[0], zr.at[slot], z_send.at[0], z_recv.at[slot], sibling).wait_recv()
-        total = zo[zi]
-        for slot in range(1, NZ):
+        for slot in range(1, 4 * NZ):
+            remote(zs.at[0, 0], zr.at[slot], z_send.at[0, 0], z_recv.at[slot], sibling).wait_recv()
+        total = zo[yh, zi]
+        for slot in range(1, 4 * NZ):
             total += zr[slot].astype(F32)[:ROWS]
         turned = pltpu.roll(total, 64, 1)
         fs[...] = jnp.where(c == 0, turned, total)
@@ -430,12 +424,9 @@
             vmem((HEADS, 4, NX, ROWS, 128), F32),
             vmem((HEADS, 3, 160, 128), BF16),
             vmem((HEADS, 3, 160, 128), BF16),
-            vmem((HEADS, 160, 128), F32),
-            vmem((HEADS, 160, 128), BF16),
-            vmem((4, 160, 128), BF16),
-            vmem((4, ROWS, 128), F32),
-            vmem((4, 48, 128), BF16),
-            vmem((NZ, 48, 128), BF16),
+            vmem((HEADS, 4, ROWS, 128), F32),
+            vmem((HEADS, 4, 48, 128), BF16),
+            vmem((4 * NZ, 48, 128), BF16),
             vmem((ROWS, 128), F32),
             vmem((ROWS, 128), F32),
             vmem((160, 128), BF16),
@@ -447,8 +438,7 @@
             dma((MEMBERS,)), dma((MEMBERS,)),
             dma((HEADS, 2)), dma((HEADS, 2)),
             dma((HEADS, 3)), dma((HEADS, 3)),
-            dma((HEADS,)), dma((4,)),
-            dma((4,)), dma((NZ,)),
+            dma((HEADS, 4)), dma((4 * NZ,)),
             dma, dma,
             dma((4,)), dma((4,)),
             dma((3,)), dma((3,)),

time: 50.1 us -> 47.9 us (0.956)
  Pallas kernels: 48 us -> 45.7 us
    pallas_call x1, Pallas kernels: 47 us -> 44.7 us  [local(): pl.pallas_call(kernel, out_shape=(vmem((ROWS, 64), F32), vmem((2, LEN, HA...]
where the time goes in v3:
time: 47.9 us; the launch traced here: 47.6 us
  Pallas kernels  45.7 us (95%)
  between operations  1.93 us (4%)
    pallas_call x1, Pallas kernels, local(): pl.pallas_call(kernel, out_shape=(vmem((ROWS, 64), F32), vmem((2, LEN, HA...  44.7 us
    pallas_call x1, Pallas kernels, local(): pl.pallas_call(store, out_shape=(jax.ShapeDtypeStruct((ROWS, 64), F32), j...  1.03 us

profile of v3, /device:TPU:1, one launch (start us, length us, event | category | flops | bytes accessed | tf_op | source)
XLA Modules:
  0.0 47.6 jit_solution(2034706115829294724)
XLA Ops:
  1.9 44.7 %shard_map.86 = (f32[40,64]{1,0:T(8,128)S(1)}, bf16[2,224,1280]{2,1,0:T(8,128)(2,1)S(1)}) custom-call(bf16[224,2560]{1,0:T(8,128)(2,1)} %bitcast.5, bf16[224,2560]{1,0:T(8,128)(2,1)} %bitcast.6, bf16[224,512]{1,0:T(8,128)(2,1)} %bitcast.8, bf16[224,2560]{1,0:T(8,128)(2,1)} %bitcast.7, s32[1,1]{1,0:T(1,128)S(6)} %copy.9.length_ref, ...), custom_call_target="tpu_custom_call" | custom-call | tf_op jit(solution)/shard_map/pallas_call | solution.py:402
  46.6 1.0 %shard_map.87 = (f32[40,64]{1,0:T(8,128)}, bf16[224,2560]{1,0:T(8,128)(2,1)}) custom-call(f32[40,64]{1,0:T(8,128)S(1)} %get-tuple-element.6.gradient, bf16[2,224,1280]{2,1,0:T(8,128)(2,1)S(1)} %get-tuple-element.7.halves), custom_call_target="tpu_custom_call" | custom-call | tf_op jit(solution)/shard_map/pallas_call | solution.py:456

commit v4 on v3

--- a/solution.py
+++ b/solution.py
@@ -59,7 +59,7 @@
     in_sem, ex_send, ex_recv, rw_send, rw_recv,
     s1_send, s1_recv, s2_send, s2_recv, z_send, z_recv, f_send, f_recv,
     wz_send, wz_recv, wx_send, wx_recv, wy_send, wy_recv,
-    ry_send, ry_recv, rx_send, rx_recv, rz_send, rz_recv, gs_send, gs_recv,
+    ro_send, ro_recv, rz_send, rz_recv, gs_send, gs_recv,
 ):
     g = lax.axis_index("grp")
     f = lax.axis_index("fsdp")
@@ -83,7 +83,8 @@
     zs_both = [at(lax.rem(z + d, NZ), x, y, k) for d in range(1, NZ) for k in range(2)]
 
     barrier = pltpu.get_barrier_semaphore()
-    partners = group + [up, down] + xs + zs_both
+    below = [at(z, lax.rem(x + d, NX), lax.rem(y + NY - 1, NY), c) for d in range(1, NX)]
+    partners = group + [up, down] + xs + zs_both + below
     for device in partners:
         pl.semaphore_signal(barrier, inc=1, device_id=device, device_id_type=MESH)
 
@@ -162,17 +163,18 @@
         def _(i=i):
             w_send(i).start()
 
-    rest_y = remote(ws.at[rest], wg.at[yl, x, zi, rest], ry_send, ry_recv, up)
-    rest_y_arrival = remote(ws.at[rest], wg.at[1 - yl, x, zi, rest], ry_send, ry_recv, up)
-    rest_x = [
-        remote(wg.at[:, x, zi, rest], wg.at[:, x, zi, rest], rx_send.at[d], rx_recv.at[d], xs[d]) for d in range(NX - 1)
+    rest_places = [(lax.rem(x + d, NX), y) for d in range(1, NX)]
+    rest_places += [(lax.rem(x + d, NX), lax.rem(y + 1, NY)) for d in range(NX)]
+    rest_out = [
+        remote(ws.at[rest], wg.at[yl, x, zi, rest], ro_send.at[n], ro_recv.at[yl, x], at(z, to_x, to_y, c))
+        for n, (to_x, to_y) in enumerate(rest_places)
     ]
-    rest_x_arrival = [
+    rest_in = [
         remote(
-            wg.at[:, x, zi, rest], wg.at[:, lax.rem(x + NX - 1 - d, NX), zi, rest],
-            rx_send.at[d], rx_recv.at[d], xs[d],
-        )
-        for d in range(NX - 1)
+            ws.at[rest], wg.at[lax.rem(to_y, 2), to_x, zi, rest], ro_send.at[n], ro_recv.at[lax.rem(to_y, 2), to_x],
+            sibling,
+        )
+        for n, (to_x, to_y) in enumerate(rest_places)
     ]
     rest_z = [
         remote(
@@ -189,7 +191,8 @@
 
     @pl.when(c == zc)
     def _():
-        rest_y.start()
+        for copy in rest_out:
+            copy.start()
 
     for j in range(1, HEADS):
         attend(j)
@@ -199,12 +202,6 @@
     for b in range(10):
         cols = slice(b * 128, (b + 1) * 128)
         ht[0, cols, :] = hb[0, :, cols].T
-
-    @pl.when(c == zc)
-    def _():
-        rest_y_arrival.wait_recv()
-        for copy in rest_x:
-            copy.start()
 
     share_h.wait_recv()
     for b in range(10):
@@ -246,13 +243,13 @@
         for copy in copies:
             copy.start()
         s1.append(copies)
-
-    @pl.when(c == zc)
-    def _():
-        for copy in rest_x_arrival:
-            copy.wait_recv()
-        for copy in rest_z:
-            copy.start()
+        if j == 0:
+            @pl.when(c == zc)
+            def _():
+                for copy in rest_in:
+                    copy.wait_recv()
+                for copy in rest_z:
+                    copy.start()
 
     for i in range(4):
         @pl.when(4 * c + i != z)
@@ -347,8 +344,7 @@
 
     @pl.when(c == zc)
     def _():
-        rest_y.wait_send()
-        for copy in rest_x + rest_z:
+        for copy in rest_out + rest_z:
             copy.wait_send()
 
     for i in range(4):
@@ -443,7 +439,7 @@
             dma((4,)), dma((4,)),
             dma((3,)), dma((3,)),
             dma((2,)), dma((2,)),
-            dma, dma, dma((3,)), dma((3,)), dma((NZ,)), dma((4,)),
+            dma((7,)), dma((2, NX)), dma((NZ,)), dma((4,)),
             dma, dma,
         ],
         compiler_params=pltpu.CompilerParams(

time: 47.9 us -> 48.1 us (level)
  no operation moved by 1% of the time
where the time goes in v4:
time: 48.1 us; the launch traced here: 47.9 us
  Pallas kernels  46 us (96%)
  between operations  1.93 us (4%)
    pallas_call x1, Pallas kernels, local(): pl.pallas_call(kernel, out_shape=(vmem((ROWS, 64), F32), vmem((2, LEN, HA...  45 us
    pallas_call x1, Pallas kernels, local(): pl.pallas_call(store, out_shape=(jax.ShapeDtypeStruct((ROWS, 64), F32), j...  1.03 us

profile of v4, /device:TPU:1, one launch (start us, length us, event | category | flops | bytes accessed | tf_op | source)
XLA Modules:
  0.0 47.9 jit_solution(12397915241279889178)
XLA Ops:
  1.9 45.0 %shard_map.86 = (f32[40,64]{1,0:T(8,128)S(1)}, bf16[2,224,1280]{2,1,0:T(8,128)(2,1)S(1)}) custom-call(bf16[224,2560]{1,0:T(8,128)(2,1)} %bitcast.5, bf16[224,2560]{1,0:T(8,128)(2,1)} %bitcast.6, bf16[224,512]{1,0:T(8,128)(2,1)} %bitcast.8, bf16[224,2560]{1,0:T(8,128)(2,1)} %bitcast.7, s32[1,1]{1,0:T(1,128)S(6)} %copy.9.length_ref, ...), custom_call_target="tpu_custom_call" | custom-call | tf_op jit(solution)/shard_map/pallas_call | solution.py:398
  46.9 1.0 %shard_map.87 = (f32[40,64]{1,0:T(8,128)}, bf16[224,2560]{1,0:T(8,128)(2,1)}) custom-call(f32[40,64]{1,0:T(8,128)S(1)} %get-tuple-element.6.gradient, bf16[2,224,1280]{2,1,0:T(8,128)(2,1)S(1)} %get-tuple-element.7.halves), custom_call_target="tpu_custom_call" | custom-call | tf_op jit(solution)/shard_map/pallas_call | solution.py:452
